TPU v7x, 32 devices: a whole 2x2x4 slice. The times are simulated.
32 devices in a mesh: dom: 16 (over z, y, x), rhs: 2 (over core).
Axes of the slice: x: 2, y: 2, z: 4, core: 2. Of those that a mesh axis runs over, the one named last changes fastest.
Arguments:
- jacobian: bfloat16 [128, 7, 162, 162], P('dom'), may hold values from -0.1875 to 0.1875
- block_weight: bfloat16 [128, 162, 162], P('dom'), may hold values from -0.5 to 0.5
- rhs_grad: float32 [128, 16, 162], P('dom', 'rhs')
- flow_residual: float32 [128, 162], P('dom'), may hold values from -6 to 6
- face_nbr: int32 [128, 6], P('dom'), may hold values from 0 to 11, as said below
- send_list: int32 [16, 2, 2], P('dom'), may hold values from 0 to 7, as said below
Outputs:
- adjoint: float32 [128, 16, 162], P('dom', 'rhs')
- residual_check: float32 [128, 16, 162], P('dom', 'rhs')
- indicator: float32 [128], P('dom')
Inputs may be any that keep to these rules, and one draw needn't show every extreme that they name: `face_nbr`: A value m < 8 names an element of the same partition; 8 + s with s < 2 names slot s of list 1 of the partition below; 10 + s names slot s of list 0 of the partition above. The first partition never uses the range below and the last never the range above. `send_list`: the 4 entries of one partition's two lists are distinct local element indices.
All inputs are finite; a program needn't handle non-finite values.
Results may differ from a plain program's by a relative error of at most 0.008.
Values may be sent and summed in bfloat16 or wider, within the bound.
A program may use at most 64 MiB of HBM per device.

v0:
```python
import jax
import jax.numpy as jnp
from jax import lax
from jax.sharding import PartitionSpec as P

ITERS = 2


epsilon = 1e-06


def padded(x, sides, width):
    for axis, dim in sides:
        devices, length = (lax.axis_size(axis), x.shape[dim])
        up = [(i, (i + 1) % devices) for i in range(devices - 1)]
        down = [(j, i) for i, j in up]
        last = lax.slice_in_dim(x, length - width, length, axis=dim)
        first = lax.slice_in_dim(x, 0, width, axis=dim)
        before = lax.ppermute(last, axis, up)
        after = lax.ppermute(first, axis, down)
        x = jnp.concatenate([before, x, after], axis=dim)
    return x


def inner(first, second):
    return jnp.sum(first * second, axis=(0, 2))


def norm_of(vectors):
    return jnp.sqrt(lax.psum(inner(vectors, vectors), "dom") + epsilon)


def least_squares(beta, hess):
    target = [beta] + [jnp.zeros_like(beta)] * ITERS
    cosines = []
    sines = []
    upper = {}
    for column in range(ITERS):
        entries = [hess[row, column] for row in range(column + 2)]
        for row in range(column):
            first = cosines[row] * entries[row] + sines[row] * entries[row + 1]
            second = -sines[row] * entries[row] + cosines[row] * entries[row + 1]
            entries[row] = first
            entries[row + 1] = second
        radius = jnp.sqrt(
            entries[column] * entries[column] + entries[column + 1] * entries[column + 1]
        )
        cosine = entries[column] / radius
        sine = entries[column + 1] / radius
        cosines.append(cosine)
        sines.append(sine)
        for row in range(column):
            upper[row, column] = entries[row]
        upper[column, column] = radius
        current = target[column]
        target[column] = cosine * current
        target[column + 1] = -sine * current
    coeffs = [jnp.zeros_like(beta)] * ITERS
    for row in reversed(range(ITERS)):
        partial_sum = target[row]
        for later in range(row + 1, ITERS):
            partial_sum = partial_sum - upper[row, later] * coeffs[later]
        coeffs[row] = partial_sum / upper[row, row]
    return coeffs


def per_device(jacobian, block_weight, rhs_grad, flow_residual, face_nbr, send_list):
    elements = jacobian.shape[0]
    capacity = send_list.shape[2]
    shared_rows = send_list[0]
    nearby = padded(shared_rows, (("dom", 0),), 1)
    prev_upper = nearby[0]
    next_lower = nearby[3]
    slots = jnp.arange(elements + 2 * capacity, dtype=jnp.int32)
    one_hot = (face_nbr[:, :, None] == slots[None, None, :]).astype(jnp.float32)

    def build_table(rounded):
        widened = padded(rounded, (("dom", 0),), elements)
        return jnp.concatenate(
            [
                rounded,
                jnp.take(widened, prev_upper, axis=0),
                jnp.take(widened, 2 * elements + next_lower, axis=0),
            ],
            axis=0,
        )

    def products(table, faces, blocks, weights, hot, rows):
        beside_all = jnp.take(table, faces, axis=0)
        stacked = jnp.concatenate([rows[:, None], beside_all], axis=1)
        image = jnp.einsum(
            "ekij,ekrj->eri", blocks, stacked, preferred_element_type=jnp.float32
        ).astype(jnp.bfloat16)
        scaled = jnp.einsum(
            "eij,erj->eri", weights, image, preferred_element_type=jnp.float32
        ).astype(jnp.bfloat16)
        terms = jnp.einsum("ekij,eri->ekrj", blocks, scaled, preferred_element_type=jnp.float32)
        count = terms.shape[0]
        rhs_count = terms.shape[2]
        width = terms.shape[3]
        flat_terms = terms[:, 1:].reshape(count, terms.shape[1] - 1, rhs_count * width)
        spread = jnp.einsum("ekn,ekm->nm", hot, flat_terms, precision=lax.Precision.HIGHEST)
        return (spread.reshape(elements + 2 * capacity, rhs_count, width), terms[:, 0])

    def operate(field):
        rounded = field.astype(jnp.bfloat16)
        table = build_table(rounded)
        spread, diagonal_terms = products(table, face_nbr, jacobian, block_weight, one_hot, rounded)
        owned = spread[:elements] + diagonal_terms
        lower_terms = spread[elements : elements + capacity]
        upper_terms = spread[elements + capacity :]
        rhs_count = owned.shape[1]
        width = owned.shape[2]
        blank = jnp.zeros((elements, rhs_count, width), jnp.float32)
        prev_part = blank.at[prev_upper].set(lower_terms)
        next_part = blank.at[next_lower].set(upper_terms)
        returned = padded(
            jnp.concatenate([prev_part, next_part], axis=0).astype(jnp.bfloat16),
            (("dom", 0),),
            elements,
        ).astype(jnp.float32)
        owned = owned + returned[:elements] + returned[3 * elements :]
        return owned

    beta = norm_of(rhs_grad)
    basis = [rhs_grad / beta[None, :, None]]
    raws = []
    hess = {}
    for column in range(ITERS):
        work = operate(basis[column])
        raws.append(work)
        factors = lax.psum(jnp.stack([inner(vector, work) for vector in basis]), "dom")
        for row in range(column + 1):
            hess[row, column] = factors[row]
            work = work - factors[row][None, :, None] * basis[row]
        length = norm_of(work)
        hess[column + 1, column] = length
        if column + 1 < ITERS:
            basis.append(work / length[None, :, None])
    coeffs = least_squares(beta, hess)
    adjoint = jnp.zeros_like(rhs_grad)
    recurrence = rhs_grad
    for column in range(ITERS):
        adjoint = adjoint + coeffs[column][None, :, None] * basis[column]
        recurrence = recurrence - coeffs[column][None, :, None] * raws[column]
    refined = adjoint + recurrence
    residual_check = rhs_grad - operate(refined)
    local_terms = jnp.sum(jnp.abs(jnp.sum(adjoint * flow_residual[:, None, :], axis=2)), axis=1)
    indicator = lax.psum(local_terms, "rhs")
    return (adjoint, residual_check, indicator)


def solution(mesh):
    in_specs = (
        P("dom", None, None, None),
        P("dom", None, None),
        P("dom", "rhs", None),
        P("dom", None),
        P("dom", None),
        P("dom", None, None),
    )
    out_specs = (P("dom", "rhs", None), P("dom", "rhs", None), P("dom"))
    return jax.shard_map(
        per_device, mesh=mesh, in_specs=in_specs, out_specs=out_specs, check_vma=False
    )
```

profile of v0, /device:TPU:0, one launch (start us, length us, event | category | flops | bytes accessed | tf_op | source)
XLA Modules:
  0.0 291.6 jit_solution(8154584523717022447)
XLA Ops:
  0.6 1.0 multiply_reduce_fusion.6
  1.7 43.5 %psum.42 = f32[8]{0:T(128)S(1)} all-reduce(f32[8]{0:T(128)S(1)} %multiply_reduce_fusion.6), channel_id=1, replica_groups=mesh['dom'=16,'rhs'=2] {'dom'}, use_global_device_ids=true, to_apply=%region_1.0 | all-reduce | flops 8 | bytes 64 | tf_op jit(solution)/shard_map/psum | solution.py:30
  45.2 0.9 fusion.73
  46.1 1.3 collective-permute-start
  47.4 1.3 collective-permute-start.1
  48.7 0.8 slice_bitcast_fusion.5
  49.4 4.5 %collective-permute-start.2 = (s32[1,2]{1,0:T(1,128)S(1)}, s32[1,2]{1,0:T(1,128)S(1)}, u32[]{:S(2)}, u32[]{:S(2)}) collective-permute-start(s32[1,2]{1,0:T(1,128)S(1)} %get-tuple-element.27), channel_id=1, source_target_pairs={{0,2},{2,4},{4,6},{6,8},{8,10},{10,12},{12,14},{14,16},{16,18},{18... | collective-permute-start | bytes 32 | tf_op jit(solution)/shard_map/ppermute | solution.py:19
  54.0 1.3 collective-permute-start.3
  55.3 0.7 compare_select_fusion
  56.0 0.7 compare_and_fusion
  56.7 0.9 fusion.86
  57.6 0.8 copy.29
  58.5 0.9 collective-permute-done.3
  59.5 0.5 gather_fusion
  60.1 0.5 gather_fusion.1
  60.8 0.6 gather_fusion.2
  61.5 3.7 %fusion.36 = bf16[8,8,162]{2,1,0:T(8,128)(2,1)S(1)} fusion(bf16[8,7,162,162]{3,0,2,1:T(8,128)(2,1)} %param.10, bf16[8,6,8,162]{3,2,1,0:T(8,128)(2,1)S(1)} %broadcast_select_fusion.2, bf16[8,1,8,162]{3,2,1,0:T(8,128)(2,1)S(1)} %fusion.86), kind=kOutput, calls=%fused_computation.38 | convolution fusion | flops 23597568 | bytes 3105216 | tf_op jit(solution)/shard_map/ekij,ekrj->eri/dot_general | solution.py:91
  65.2 4.0 %fusion.12 = f32[8,7,8,162]{3,2,0,1:T(8,128)S(1)} fusion(bf16[8,7,162,162]{3,0,2,1:T(8,128)(2,1)} %param.10, bf16[8,8,162]{2,1,0:T(8,128)(2,1)S(1)} %fusion.36, bf16[8,162,162]{2,0,1:T(8,128)(2,1)S(1)} %copy-done), kind=kOutput, calls=%fused_computation.30 | convolution fusion | flops 26884224 | bytes 3670272 | tf_op jit(solution)/shard_map/ekij,eri->ekrj/dot_general | solution.py:97
  69.2 0.2 reshape.106
  69.4 0.3 convolution_bitcast_fusion.2
  69.8 0.6 scatter_fusion.1
  70.5 1.3 collective-permute-start.5
  71.9 0.6 scatter_fusion
  72.5 4.5 %collective-permute-start.4 = (bf16[8,8,162]{2,1,0:T(8,128)(2,1)S(1)}, bf16[8,8,162]{2,1,0:T(8,128)(2,1)S(1)}, u32[]{:S(2)}, u32[]{:S(2)}) collective-permute-start(bf16[8,8,162]{2,1,0:T(8,128)(2,1)S(1)} %slice.138), channel_id=1, source_target_pairs={{0,2},{2,4},{4,6},{6,8},{8,10},{10,12},{12,14},{14,16},{16,18},{18... | collective-permute-start | bytes 62216 | tf_op jit(solution)/shard_map/ppermute | solution.py:19
  77.2 1.5 collective-permute-done.4
  78.6 0.2 multiply_reduce_fusion.5
  78.8 40.4 %psum.43 = f32[8]{0:T(128)S(1)} all-reduce(f32[8]{0:T(128)S(1)} %get-tuple-element.14), channel_id=1, replica_groups=mesh['dom'=16,'rhs'=2] {'dom'}, use_global_device_ids=true, to_apply=%region_5.8 | all-reduce | flops 8 | bytes 64 | tf_op jit(solution)/shard_map/psum | solution.py:132
  119.2 0.2 multiply_reduce_fusion.4
  119.4 36.6 %psum.44 = f32[8]{0:T(128)S(1)} all-reduce(f32[8]{0:T(128)S(1)} %multiply_reduce_fusion.4), channel_id=1, replica_groups=mesh['dom'=16,'rhs'=2] {'dom'}, use_global_device_ids=true, to_apply=%region_7.10 | all-reduce | flops 8 | bytes 64 | tf_op jit(solution)/shard_map/psum | solution.py:30
  156.1 3.9 %collective-permute-start.6 = (bf16[8,8,162]{2,1,0:T(8,128)(2,1)S(1)}, bf16[8,8,162]{2,1,0:T(8,128)(2,1)S(1)}, u32[]{:S(2)}, u32[]{:S(2)}) collective-permute-start(bf16[8,8,162]{2,1,0:T(8,128)(2,1)S(1)} %get-tuple-element.12), channel_id=1, source_target_pairs={{0,2},{2,4},{4,6},{6,8},{8,10},{10,12},{12,14},{14,16},{16,18},{18... | collective-permute-start | bytes 62216 | tf_op jit(solution)/shard_map/ppermute | solution.py:19
  160.0 1.3 collective-permute-start.7
  161.3 0.3 collective-permute-done.6
  161.6 4.2 %collective-permute-done.7 = bf16[8,8,162]{2,1,0:T(8,128)(2,1)S(1)} collective-permute-done((bf16[8,8,162]{2,1,0:T(8,128)(2,1)S(1)}, bf16[8,8,162]{2,1,0:T(8,128)(2,1)S(1)}, u32[]{:S(2)}, u32[]{:S(2)}) %collective-permute-start.7) | collective-permute-done | bytes 20768 | tf_op jit(solution)/shard_map/ppermute | solution.py:20
  165.8 0.5 gather_fusion.3
  166.4 0.5 gather_fusion.4
  167.0 0.6 gather_fusion.5
  167.8 3.7 %fusion.33 = bf16[8,8,162]{2,1,0:T(8,128)(2,1)S(1)} fusion(bf16[8,7,162,162]{3,0,2,1:T(8,128)(2,1)} %param.10, bf16[8,6,8,162]{3,2,1,0:T(8,128)(2,1)S(1)} %broadcast_select_fusion.1, bf16[8,1,8,162]{3,2,1,0:T(8,128)(2,1)S(1)} %bitcast.127), kind=kOutput, calls=%fused_computation.37 | convolution fusion | flops 23597568 | bytes 3105216 | tf_op jit(solution)/shard_map/ekij,ekrj->eri/dot_general | solution.py:91
  171.4 4.0 %fusion.15 = f32[8,7,8,162]{3,2,0,1:T(8,128)S(1)} fusion(bf16[8,7,162,162]{3,0,2,1:T(8,128)(2,1)} %param.10, bf16[8,8,162]{2,1,0:T(8,128)(2,1)S(1)} %fusion.33, bf16[8,162,162]{2,0,1:T(8,128)(2,1)S(1)} %copy-done), kind=kOutput, calls=%fused_computation.31 | convolution fusion | flops 26884224 | bytes 3670272 | tf_op jit(solution)/shard_map/ekij,eri->ekrj/dot_general | solution.py:97
  175.6 0.3 convolution_bitcast_fusion.1
  176.1 0.6 scatter_fusion.2
  176.7 2.8 collective-permute-start.8
  179.6 0.6 scatter_fusion.3
  180.3 1.3 collective-permute-start.9
  181.7 4.4 %collective-permute-done.9 = bf16[8,8,162]{2,1,0:T(8,128)(2,1)S(1)} collective-permute-done((bf16[8,8,162]{2,1,0:T(8,128)(2,1)S(1)}, bf16[8,8,162]{2,1,0:T(8,128)(2,1)S(1)}, u32[]{:S(2)}, u32[]{:S(2)}) %collective-permute-start.9) | collective-permute-done | bytes 20768 | tf_op jit(solution)/shard_map/ppermute | solution.py:20
  186.1 0.2 multiply_reduce_fusion.3
  186.3 37.5 %psum.45 = f32[2,8]{1,0:T(2,128)S(1)} all-reduce(f32[2,8]{1,0:T(2,128)S(1)} %pad_maximum_fusion.15), channel_id=1, replica_groups=mesh['dom'=16,'rhs'=2] {'dom'}, use_global_device_ids=true, to_apply=%region_12.15 | all-reduce | flops 16 | bytes 128 | tf_op jit(solution)/shard_map/psum | solution.py:132
  223.8 0.2 multiply_reduce_fusion.1
  224.0 37.6 %psum.46 = f32[8]{0:T(128)S(1)} all-reduce(f32[8]{0:T(128)S(1)} %multiply_reduce_fusion.1), channel_id=1, replica_groups=mesh['dom'=16,'rhs'=2] {'dom'}, use_global_device_ids=true, to_apply=%region_14.17 | all-reduce | flops 8 | bytes 64 | tf_op jit(solution)/shard_map/psum | solution.py:30
  262.0 2.9 collective-permute-start.10
  264.8 1.5 collective-permute-start.11
  266.4 4.2 %collective-permute-done.11 = bf16[8,8,162]{2,1,0:T(8,128)(2,1)S(1)} collective-permute-done((bf16[8,8,162]{2,1,0:T(8,128)(2,1)S(1)}, bf16[8,8,162]{2,1,0:T(8,128)(2,1)S(1)}, u32[]{:S(2)}, u32[]{:S(2)}) %collective-permute-start.11) | collective-permute-done | bytes 20768 | tf_op jit(solution)/shard_map/ppermute | solution.py:20
  270.7 0.5 gather_fusion.6
  271.2 0.5 gather_fusion.7
  271.9 0.6 gather_fusion.8
  272.7 3.7 %fusion.30 = bf16[8,8,162]{2,1,0:T(8,128)(2,1)S(1)} fusion(bf16[8,7,162,162]{3,0,2,1:T(8,128)(2,1)} %param.10, bf16[8,6,8,162]{3,2,1,0:T(8,128)(2,1)S(1)} %broadcast_select_fusion, bf16[8,1,8,162]{3,2,1,0:T(8,128)(2,1)S(1)} %bitcast.126), kind=kOutput, calls=%fused_computation.36 | convolution fusion | flops 23597568 | bytes 3105216 | tf_op jit(solution)/shard_map/ekij,ekrj->eri/dot_general | solution.py:91
  276.3 3.9 %fusion.18 = f32[8,7,8,162]{3,2,0,1:T(8,128)S(1)} fusion(bf16[8,7,162,162]{3,0,2,1:T(8,128)(2,1)} %param.10, bf16[8,8,162]{2,1,0:T(8,128)(2,1)S(1)} %fusion.30, bf16[8,162,162]{2,0,1:T(8,128)(2,1)S(1)} %copy-done), kind=kOutput, calls=%fused_computation.32 | convolution fusion | flops 26884224 | bytes 3670272 | tf_op jit(solution)/shard_map/ekij,eri->ekrj/dot_general | solution.py:97
  280.5 0.3 convolution_bitcast_fusion
  281.0 0.6 scatter_fusion.4
  281.6 2.8 collective-permute-start.12
  284.5 0.6 scatter_fusion.5
  285.1 1.3 collective-permute-start.13
  286.5 3.0 %psum.47 = f32[8]{0:T(128)} all-reduce(f32[8]{0:T(128)S(1)} %abs_reduce_fusion), channel_id=1, replica_groups=mesh['dom'=16,'rhs'=2] {'rhs'}, use_global_device_ids=true, to_apply=%region_19.22 | all-reduce | flops 8 | bytes 64 | tf_op jit(solution)/shard_map/psum | solution.py:149
  289.6 1.3 collective-permute-done.13
  290.9 0.7 fusion.58
  (79 shorter events, 3.0 us)
Async XLA Ops:
  0.6 64.5 %copy-start = (bf16[8,162,162]{2,0,1:T(8,128)(2,1)S(1)}, bf16[8,162,162]{2,0,1:T(8,128)(2,1)}, u32[]{:S(2)}) copy-start(bf16[8,162,162]{2,0,1:T(8,128)(2,1)} %param.11) | copy-start | bytes 1259716
  46.1 13.4 %collective-permute-start = (bf16[8,8,162]{2,1,0:T(8,128)(2,1)S(1)}, bf16[8,8,162]{2,1,0:T(8,128)(2,1)S(1)}, u32[]{:S(2)}, u32[]{:S(2)}) collective-permute-start(bf16[8,8,162]{2,1,0:T(8,128)(2,1)S(1)} %fusion.73), channel_id=1, source_target_pairs={{0,2},{2,4},{4,6},{6,8},{8,10},{10,12},{12,14},{14,16},{16,18},{18... | collective-permute-start | bytes 62216 | tf_op jit(solution)/shard_map/ppermute | solution.py:19
  47.4 12.1 %collective-permute-start.1 = (bf16[8,8,162]{2,1,0:T(8,128)(2,1)S(1)}, bf16[8,8,162]{2,1,0:T(8,128)(2,1)S(1)}, u32[]{:S(2)}, u32[]{:S(2)}) collective-permute-start(bf16[8,8,162]{2,1,0:T(8,128)(2,1)S(1)} %fusion.73), channel_id=1, source_target_pairs={{2,0},{4,2},{6,4},{8,6},{10,8},{12,10},{14,12},{16,14},{18,16},{20... | collective-permute-start | bytes 62216 | tf_op jit(solution)/shard_map/ppermute | solution.py:20
  49.4 9.0 %collective-permute-start.2 = (s32[1,2]{1,0:T(1,128)S(1)}, s32[1,2]{1,0:T(1,128)S(1)}, u32[]{:S(2)}, u32[]{:S(2)}) collective-permute-start(s32[1,2]{1,0:T(1,128)S(1)} %get-tuple-element.27), channel_id=1, source_target_pairs={{0,2},{2,4},{4,6},{6,8},{8,10},{10,12},{12,14},{14,16},{16,18},{18... | collective-permute-start | bytes 32 | tf_op jit(solution)/shard_map/ppermute | solution.py:19
  54.0 5.4 %collective-permute-start.3 = (s32[1,2]{1,0:T(1,128)S(1)}, s32[1,2]{1,0:T(1,128)S(1)}, u32[]{:S(2)}, u32[]{:S(2)}) collective-permute-start(s32[1,2]{1,0:T(1,128)S(1)} %get-tuple-element.26), channel_id=1, source_target_pairs={{2,0},{4,2},{6,4},{8,6},{10,8},{12,10},{14,12},{16,14},{18,16},{20... | collective-permute-start | bytes 32 | tf_op jit(solution)/shard_map/ppermute | solution.py:20
  65.2 13.5 %copy-start.1 = (f32[8,8,162]{2,1,0:T(8,128)S(1)}, f32[8,8,162]{2,1,0:T(8,128)}, u32[]{:S(2)}) copy-start(f32[8,8,162]{2,1,0:T(8,128)} %param.12) | copy-start | bytes 124420
  70.5 6.7 %collective-permute-start.5 = (bf16[8,8,162]{2,1,0:T(8,128)(2,1)S(1)}, bf16[8,8,162]{2,1,0:T(8,128)(2,1)S(1)}, u32[]{:S(2)}, u32[]{:S(2)}) collective-permute-start(bf16[8,8,162]{2,1,0:T(8,128)(2,1)S(1)} %slice.141), channel_id=1, source_target_pairs={{2,0},{4,2},{6,4},{8,6},{10,8},{12,10},{14,12},{16,14},{18,16},{20... | collective-permute-start | bytes 62216 | tf_op jit(solution)/shard_map/ppermute | solution.py:20
  72.5 6.1 %collective-permute-start.4 = (bf16[8,8,162]{2,1,0:T(8,128)(2,1)S(1)}, bf16[8,8,162]{2,1,0:T(8,128)(2,1)S(1)}, u32[]{:S(2)}, u32[]{:S(2)}) collective-permute-start(bf16[8,8,162]{2,1,0:T(8,128)(2,1)S(1)} %slice.138), channel_id=1, source_target_pairs={{0,2},{2,4},{4,6},{6,8},{8,10},{10,12},{12,14},{14,16},{16,18},{18... | collective-permute-start | bytes 62216 | tf_op jit(solution)/shard_map/ppermute | solution.py:19
  156.1 5.5 %collective-permute-start.6 = (bf16[8,8,162]{2,1,0:T(8,128)(2,1)S(1)}, bf16[8,8,162]{2,1,0:T(8,128)(2,1)S(1)}, u32[]{:S(2)}, u32[]{:S(2)}) collective-permute-start(bf16[8,8,162]{2,1,0:T(8,128)(2,1)S(1)} %get-tuple-element.12), channel_id=1, source_target_pairs={{0,2},{2,4},{4,6},{6,8},{8,10},{10,12},{12,14},{14,16},{16,18},{18... | collective-permute-start | bytes 62216 | tf_op jit(solution)/shard_map/ppermute | solution.py:19
  160.0 5.8 %collective-permute-start.7 = (bf16[8,8,162]{2,1,0:T(8,128)(2,1)S(1)}, bf16[8,8,162]{2,1,0:T(8,128)(2,1)S(1)}, u32[]{:S(2)}, u32[]{:S(2)}) collective-permute-start(bf16[8,8,162]{2,1,0:T(8,128)(2,1)S(1)} %get-tuple-element.12), channel_id=1, source_target_pairs={{2,0},{4,2},{6,4},{8,6},{10,8},{12,10},{14,12},{16,14},{18,16},{20... | collective-permute-start | bytes 62216 | tf_op jit(solution)/shard_map/ppermute | solution.py:20
  171.4 90.2 %copy-start.3 = (f32[8,162]{1,0:T(8,128)S(1)}, f32[8,162]{1,0:T(8,128)}, u32[]{:S(2)}) copy-start(f32[8,162]{1,0:T(8,128)} %param.13) | copy-start | bytes 15556
  176.7 5.0 %collective-permute-start.8 = (bf16[8,8,162]{2,1,0:T(8,128)(2,1)S(1)}, bf16[8,8,162]{2,1,0:T(8,128)(2,1)S(1)}, u32[]{:S(2)}, u32[]{:S(2)}) collective-permute-start(bf16[8,8,162]{2,1,0:T(8,128)(2,1)S(1)} %slice.150), channel_id=1, source_target_pairs={{0,2},{2,4},{4,6},{6,8},{8,10},{10,12},{12,14},{14,16},{16,18},{18... | collective-permute-start | bytes 62216 | tf_op jit(solution)/shard_map/ppermute | solution.py:19
  180.3 5.8 %collective-permute-start.9 = (bf16[8,8,162]{2,1,0:T(8,128)(2,1)S(1)}, bf16[8,8,162]{2,1,0:T(8,128)(2,1)S(1)}, u32[]{:S(2)}, u32[]{:S(2)}) collective-permute-start(bf16[8,8,162]{2,1,0:T(8,128)(2,1)S(1)} %slice.153), channel_id=1, source_target_pairs={{2,0},{4,2},{6,4},{8,6},{10,8},{12,10},{14,12},{16,14},{18,16},{20... | collective-permute-start | bytes 62216 | tf_op jit(solution)/shard_map/ppermute | solution.py:20
  261.9 18.4 %copy-start.2 = (f32[8,8,162]{2,1,0:T(8,128)}, f32[8,8,162]{2,1,0:T(8,128)S(1)}, u32[]{:S(2)}) copy-start(f32[8,8,162]{2,1,0:T(8,128)S(1)} %get-tuple-element.8) | copy-start | bytes 124420
  262.0 4.4 %collective-permute-start.10 = (bf16[8,8,162]{2,1,0:T(8,128)(2,1)S(1)}, bf16[8,8,162]{2,1,0:T(8,128)(2,1)S(1)}, u32[]{:S(2)}, u32[]{:S(2)}) collective-permute-start(bf16[8,8,162]{2,1,0:T(8,128)(2,1)S(1)} %add_convert_fusion), channel_id=1, source_target_pairs={{0,2},{2,4},{4,6},{6,8},{8,10},{10,12},{12,14},{14,16},{16,18},{18... | collective-permute-start | bytes 62216 | tf_op jit(solution)/shard_map/ppermute | solution.py:19
  264.8 5.8 %collective-permute-start.11 = (bf16[8,8,162]{2,1,0:T(8,128)(2,1)S(1)}, bf16[8,8,162]{2,1,0:T(8,128)(2,1)S(1)}, u32[]{:S(2)}, u32[]{:S(2)}) collective-permute-start(bf16[8,8,162]{2,1,0:T(8,128)(2,1)S(1)} %add_convert_fusion), channel_id=1, source_target_pairs={{2,0},{4,2},{6,4},{8,6},{10,8},{12,10},{14,12},{16,14},{18,16},{20... | collective-permute-start | bytes 62216 | tf_op jit(solution)/shard_map/ppermute | solution.py:20
  281.6 8.0 %collective-permute-start.12 = (bf16[8,8,162]{2,1,0:T(8,128)(2,1)S(1)}, bf16[8,8,162]{2,1,0:T(8,128)(2,1)S(1)}, u32[]{:S(2)}, u32[]{:S(2)}) collective-permute-start(bf16[8,8,162]{2,1,0:T(8,128)(2,1)S(1)} %slice.164), channel_id=1, source_target_pairs={{0,2},{2,4},{4,6},{6,8},{8,10},{10,12},{12,14},{14,16},{16,18},{18... | collective-permute-start | bytes 62216 | tf_op jit(solution)/shard_map/ppermute | solution.py:19
  285.1 5.8 %collective-permute-start.13 = (bf16[8,8,162]{2,1,0:T(8,128)(2,1)S(1)}, bf16[8,8,162]{2,1,0:T(8,128)(2,1)S(1)}, u32[]{:S(2)}, u32[]{:S(2)}) collective-permute-start(bf16[8,8,162]{2,1,0:T(8,128)(2,1)S(1)} %slice.167), channel_id=1, source_target_pairs={{2,0},{4,2},{6,4},{8,6},{10,8},{12,10},{14,12},{16,14},{18,16},{20... | collective-permute-start | bytes 62216 | tf_op jit(solution)/shard_map/ppermute | solution.py:20
where the time goes:
time: 293 us; the launch traced here: 292 us
  blocking collectives  199 us (68%)
  starting transfers between devices  32 us (11%)
  matrix products  23.8 us (8%)
  waiting for transfers between devices  16.9 us (6%)
  local copies, waits for them, and re-layouts  11.8 us (4%)
  other arithmetic  7.19 us (2%)
    psum x3, blocking collectives, norm_of(): return jnp.sqrt(lax.psum(inner(vectors, vectors), 'dom') + epsilon)  118 us
    psum x2, blocking collectives, per_device(): lax.psum(jnp.stack([inner(vector, work) for vector in basis]), 'dom')  77.9 us
    ppermute x7, starting transfers between devices, padded(): before = lax.ppermute(last, axis, up)  22.8 us
    ppermute x7, waiting for transfers between devices, padded(): after = lax.ppermute(first, axis, down)  15.1 us
    dot_general x3, matrix products, products(): jnp.einsum('ekij,eri->ekrj', blocks, scaled, preferred_element_type=jnp.f...  11.9 us
    dot_general x3, matrix products, products(): jnp.einsum('ekij,ekrj->eri', blocks, stacked, preferred_element_type=jnp....  11 us
    ppermute x7, starting transfers between devices, padded(): after = lax.ppermute(first, axis, down)  9.23 us
  transfers between devices with their start and end apart: 14, of which 8 were waited for; matrix products, arithmetic and copies ran while one was open for 2% of the time, Pallas kernels for 0%

commit v1 on v0

v1 whole, which is shorter than its diff:
```python
import functools

import jax
import jax.numpy as jnp
from jax import lax
from jax.experimental import pallas as pl
from jax.experimental.pallas import tpu as pltpu
from jax.sharding import PartitionSpec as P

EPSILON = 1e-06
MESH = pl.DeviceIdType.MESH
F32 = jnp.float32
BF16 = jnp.bfloat16


def radices_of(n):
    out = []
    while n > 1:
        for r in (4, 2, 3, 5, 7):
            if n % r == 0:
                out.append(r)
                n //= r
                break
        else:
            out.append(n)
            n = 1
    return out


def dot_rows(rows, block):
    return lax.dot_general(rows, block, (((1,), (0,)), ((), ())), preferred_element_type=F32)


def dot_rows_t(rows, block):
    return lax.dot_general(rows, block, (((1,), (1,)), ((), ())), preferred_element_type=F32)


def coefficients(beta, b, c, d, e, f, g):
    h11 = c
    w_sq = d - 2.0 * h11 * c + h11 * h11 * b
    h21 = jnp.sqrt(jnp.maximum(w_sq, 0.0) + EPSILON)
    s = 1.0 / h21
    h12 = s * (e - h11 * c)
    v2v1 = s * (c - h11 * b)
    v2v2 = s * s * w_sq
    v2raw2 = s * s * (f - h11 * d - h11 * e + h11 * h11 * c)
    raw2sq = s * s * (g - 2.0 * h11 * f + h11 * h11 * d)
    h22 = v2raw2 - h12 * v2v1
    last = (
        raw2sq
        + h12 * h12 * b
        + h22 * h22 * v2v2
        - 2.0 * h12 * h12
        - 2.0 * h22 * v2raw2
        + 2.0 * h12 * h22 * v2v1
    )
    h32 = jnp.sqrt(jnp.maximum(last, 0.0) + EPSILON)
    radius = jnp.sqrt(h11 * h11 + h21 * h21)
    cos1, sin1 = h11 / radius, h21 / radius
    t1, t2 = cos1 * beta, -sin1 * beta
    upper = cos1 * h12 + sin1 * h22
    low = -sin1 * h12 + cos1 * h22
    radius2 = jnp.sqrt(low * low + h32 * h32)
    t2 = (low / radius2) * t2
    c2 = t2 / radius2
    c1 = (t1 - upper * c2) / radius
    return c1 - c2 * s * h11, c2 * s


def kernel(
    n, radices,
    jac_hbm, wgt_hbm, rhs_ref, flow_ref, nbr_ref, list_ref,
    adj_ref, res_ref, ind_ref,
    jac, wgt, xs, up, hsend, hrecv, asend, arecv, isend, irecv,
    jsem, wsem, hs_sem, hr_sem, as_sem, ar_sem, is_sem, ir_sem,
):
    elements, faces1 = jac.shape[0], jac.shape[1]
    cap = list_ref.shape[2]
    slots = elements + 2 * cap
    me = lax.axis_index("dom")
    core = lax.axis_index("rhs")
    cores = lax.axis_size("rhs")

    jcopies = [pltpu.make_async_copy(jac_hbm.at[e], jac.at[e], jsem.at[e]) for e in range(elements)]
    wcopy = pltpu.make_async_copy(wgt_hbm, wgt, wsem)
    for copy in jcopies:
        copy.start()
    wcopy.start()

    strides = []
    stride = 1
    for radix in radices:
        strides.append(stride)
        stride *= radix

    def partner(stage, offset):
        radix, step = radices[stage], strides[stage]
        digit = lax.rem(lax.div(me, step), radix)
        return me + (lax.rem(digit + offset, radix) - digit) * step

    barrier = pltpu.get_barrier_semaphore()
    total = cores - 1
    for stage, radix in enumerate(radices):
        for offset in range(1, radix):
            pl.semaphore_signal(barrier, inc=1, device_id=(partner(stage, offset), core), device_id_type=MESH)
            total += 1
    for o in range(1, cores):
        pl.semaphore_signal(barrier, inc=1, device_id=(me, lax.rem(core + o, cores)), device_id_type=MESH)

    @pl.when(me > 0)
    def _():
        pl.semaphore_signal(barrier, inc=1, device_id=(me - 1, core), device_id_type=MESH)

    @pl.when(me < n - 1)
    def _():
        pl.semaphore_signal(barrier, inc=1, device_id=(me + 1, core), device_id_type=MESH)

    rows_shape = rhs_ref.shape[1:]

    @pl.when(me == 0)
    def _():
        hrecv[:, 0] = jnp.zeros((4, 2 * cap) + rows_shape, F32)

    @pl.when(me == n - 1)
    def _():
        hrecv[:, 1] = jnp.zeros((4, 2 * cap) + rows_shape, F32)

    lists = [[list_ref[0, side, s] for s in range(cap)] for side in range(2)]
    nbr = [[nbr_ref[e, k] for k in range(faces1 - 1)] for e in range(elements)]

    ranges = ((0, cap), (0, 2 * cap), (0, 2 * cap), (cap, cap))

    def halo(t, side):
        first, count = ranges[t]
        target = me - 1 if side == 0 else me + 1
        return pltpu.make_async_remote_copy(
            src_ref=hsend.at[t, side, pl.ds(first, count)],
            dst_ref=hrecv.at[t, 1 - side, pl.ds(first, count)],
            send_sem=hs_sem.at[t, side],
            recv_sem=hr_sem.at[t, 1 - side],
            device_id=(target, core),
            device_id_type=MESH,
        )

    def halo_start(t):
        @pl.when(me > 0)
        def _():
            halo(t, 0).start()

        @pl.when(me < n - 1)
        def _():
            halo(t, 1).start()

    def halo_wait(t):
        @pl.when(me > 0)
        def _():
            halo(t, 1).wait_recv()

        @pl.when(me < n - 1)
        def _():
            halo(t, 0).wait_recv()

    def halo_finish(t):
        @pl.when(me > 0)
        def _():
            halo(t, 0).wait_send()

        @pl.when(me < n - 1)
        def _():
            halo(t, 1).wait_send()

    def reduce_copies(q, stage):
        return [
            pltpu.make_async_remote_copy(
                src_ref=asend.at[q, stage],
                dst_ref=arecv.at[q, stage, o - 1],
                send_sem=as_sem.at[q, stage, o - 1],
                recv_sem=ar_sem.at[q, stage, o - 1],
                device_id=(partner(stage, o), core),
                device_id_type=MESH,
            )
            for o in range(1, radices[stage])
        ]

    def reduce_start(q, stage, value):
        asend[q, stage] = value
        for copy in reduce_copies(q, stage):
            copy.start()

    def reduce_end(q, stage):
        for copy in reduce_copies(q, stage):
            copy.wait()
        value = asend[q, stage]
        for o in range(1, radices[stage]):
            value = value + arecv[q, stage, o - 1]
        return value

    stages = len(radices)
    lane = lax.broadcasted_iota(jnp.int32, asend.shape[2:], 1)

    def packed(columns):
        out = jnp.zeros(asend.shape[2:], F32)
        for i, column in enumerate(columns):
            out = jnp.where(lane == i, column, out)
        return out

    def inner(pairs):
        acc = None
        for a, b in pairs:
            acc = a * b if acc is None else acc + a * b
        return jnp.sum(acc, axis=1, keepdims=True)

    r = [rhs_ref[e] for e in range(elements)]
    b_part = packed([inner([(v, v) for v in r])])
    for side in range(2):
        for s in range(cap):
            hsend[0, side, s] = rhs_ref[lists[side][s]]
    for e in range(elements):
        xs[0, e] = r[e]

    pl.semaphore_wait(barrier, total + jnp.where(me > 0, 1, 0) + jnp.where(me < n - 1, 1, 0))
    halo_start(0)
    reduce_start(0, 0, b_part)

    def forward(t, wait_blocks=False):
        y = []
        for e in range(elements):
            if wait_blocks:
                jcopies[e].wait()
            acc = dot_rows_t(xs[t, e].astype(BF16), jac[e, 0])
            for k in range(1, faces1):
                acc = acc + dot_rows_t(xs[t, nbr[e][k - 1]].astype(BF16), jac[e, k])
            y.append(acc.astype(BF16))
        if wait_blocks:
            wcopy.wait()
        return [dot_rows_t(y[e], wgt[e]).astype(BF16) for e in range(elements)]

    def backward(z):
        acc = [jnp.zeros(rows_shape, F32) for _ in range(slots)]
        for e in range(elements):
            acc[e] = acc[e] + dot_rows(z[e], jac[e, 0])
            for k in range(1, faces1):
                term = dot_rows(z[e], jac[e, k])
                for m in range(slots):
                    acc[m] = acc[m] + jnp.where(nbr[e][k - 1] == m, term, 0.0)
        return acc

    def send_partials(t, acc):
        for m in range(slots):
            up[t, m] = acc[m]
        for side in range(2):
            for s in range(cap):
                if t < 3:
                    hsend[t, side, s] = up[t, lists[side][s]]
                hsend[t, side, cap + s] = acc[elements + side * cap + s]
        halo_start(t)

    def merged(t, m):
        value = up[t, m]
        for side in range(2):
            for s in range(cap):
                value = value + jnp.where(lists[side][s] == m, hrecv[t, side, cap + s], 0.0)
        return value

    def receive_partials(t):
        for m in range(elements):
            xs[t, m] = merged(t, m)
        for side in range(2):
            for s in range(cap):
                m = elements + side * cap + s
                xs[t, m] = up[t, m] + hrecv[t, side, s]

    halo_wait(0)
    for side in range(2):
        for s in range(cap):
            xs[0, elements + side * cap + s] = hrecv[0, side, s]
    z = forward(0, True)
    for stage in range(stages - 1):
        reduce_start(0, stage + 1, reduce_end(0, stage))
    acc = backward(z)
    b_sum = reduce_end(0, stages - 1)[:, 0:1]
    beta = jnp.sqrt(b_sum + EPSILON)
    scale = 1.0 / beta
    send_partials(1, [a * scale for a in acc])
    halo_wait(1)
    receive_partials(1)
    acc = backward(forward(1))
    send_partials(2, acc)
    halo_wait(2)
    receive_partials(2)
    span = range(elements)
    v1 = [rhs_ref[e] * scale for e in span]
    raw = [xs[1, e] for e in span]
    u2 = [xs[2, e] for e in span]
    grams = packed(
        [
            inner(zip(v1, raw)),
            inner(zip(raw, raw)),
            inner(zip(v1, u2)),
            inner(zip(raw, u2)),
            inner(zip(u2, u2)),
        ]
    )
    reduce_start(1, 0, grams)
    z = forward(2)
    for stage in range(stages - 1):
        reduce_start(1, stage + 1, reduce_end(1, stage))
    acc = backward(z)
    send_partials(3, acc)
    sums = reduce_end(1, stages - 1)
    c, d, e_, f, g = [sums[:, i : i + 1] for i in range(5)]
    a0, a1 = coefficients(beta, b_sum * scale * scale, c, d, e_, f, g)
    a0s = a0 * scale
    ind = jnp.zeros(isend.shape[1:], F32)
    ilane = lax.broadcasted_iota(jnp.int32, isend.shape[1:], 1)
    for e in span:
        adjoint = a0s * rhs_ref[e] + a1 * xs[1, e]
        adj_ref[e] = adjoint
        term = jnp.abs(jnp.sum(adjoint * flow_ref[pl.ds(e, 1), :], axis=1, keepdims=True))
        ind = jnp.where(ilane == e, jnp.sum(term, axis=0, keepdims=True), ind)
    isend[0] = ind
    icopies = [
        pltpu.make_async_remote_copy(
            src_ref=isend.at[0],
            dst_ref=irecv.at[o - 1],
            send_sem=is_sem.at[o - 1],
            recv_sem=ir_sem.at[o - 1],
            device_id=(me, lax.rem(core + o, cores)),
            device_id_type=MESH,
        )
        for o in range(1, cores)
    ]
    for copy in icopies:
        copy.start()
    k1 = beta + a0
    k2 = a1 - a0
    halo_wait(3)
    for e in span:
        res_ref[e] = rhs_ref[e] - (k1 * xs[1, e] + k2 * xs[2, e] - a1 * merged(3, e))
    for copy in icopies:
        copy.wait()
    for o in range(1, cores):
        ind = ind + irecv[o - 1]
    ind_ref[...] = ind[0:1, 0:elements]
    for t in range(4):
        halo_finish(t)


def per_device(n, jacobian, block_weight, rhs_grad, flow_residual, face_nbr, send_list):
    elements = jacobian.shape[0]
    rows = rhs_grad.shape[1:]
    cap = send_list.shape[2]
    slots = elements + 2 * cap
    radices = radices_of(n)
    stages, widest = len(radices), max(radices)
    cores = lax.axis_size("rhs")
    vmem = pl.BlockSpec(memory_space=pltpu.VMEM)
    smem = pl.BlockSpec(memory_space=pltpu.SMEM)
    anywhere = pl.BlockSpec(memory_space=pl.ANY)
    adjoint, residual, indicator = pl.pallas_call(
        functools.partial(kernel, n, radices),
        out_shape=(
            jax.ShapeDtypeStruct(rhs_grad.shape, F32),
            jax.ShapeDtypeStruct(rhs_grad.shape, F32),
            jax.ShapeDtypeStruct((1, elements), F32),
        ),
        in_specs=[anywhere, anywhere, vmem, vmem, smem, smem],
        out_specs=(vmem, vmem, vmem),
        scratch_shapes=[
            pltpu.VMEM(jacobian.shape, BF16),
            pltpu.VMEM(block_weight.shape, BF16),
            pltpu.VMEM((3, slots) + rows, F32),
            pltpu.VMEM((4, slots) + rows, F32),
            pltpu.VMEM((4, 2, 2 * cap) + rows, F32),
            pltpu.VMEM((4, 2, 2 * cap) + rows, F32),
            pltpu.VMEM((2, stages, rows[0], 128), F32),
            pltpu.VMEM((2, stages, widest - 1, rows[0], 128), F32),
            pltpu.VMEM((1, 8, 128), F32),
            pltpu.VMEM((max(cores - 1, 1), 8, 128), F32),
            pltpu.SemaphoreType.DMA((elements,)),
            pltpu.SemaphoreType.DMA,
            pltpu.SemaphoreType.DMA((4, 2)),
            pltpu.SemaphoreType.DMA((4, 2)),
            pltpu.SemaphoreType.DMA((2, stages, widest - 1)),
            pltpu.SemaphoreType.DMA((2, stages, widest - 1)),
            pltpu.SemaphoreType.DMA((max(cores - 1, 1),)),
            pltpu.SemaphoreType.DMA((max(cores - 1, 1),)),
        ],
        compiler_params=pltpu.CompilerParams(
            collective_id=0, has_side_effects=True, vmem_limit_bytes=40 * 2**20
        ),
    )(jacobian, block_weight, rhs_grad, flow_residual, face_nbr, send_list)
    return adjoint, residual, indicator.reshape(elements)


def solution(mesh):
    in_specs = (
        P("dom", None, None, None),
        P("dom", None, None),
        P("dom", "rhs", None),
        P("dom", None),
        P("dom", None),
        P("dom", None, None),
    )
    out_specs = (P("dom", "rhs", None), P("dom", "rhs", None), P("dom"))
    return jax.shard_map(
        functools.partial(per_device, mesh.shape["dom"]),
        mesh=mesh,
        in_specs=in_specs,
        out_specs=out_specs,
        check_vma=False,
    )
```

time: 293 us -> 43.3 us (0.15)
  blocking collectives: 199 us -> 0 us
  Pallas kernels: 0 us -> 36.1 us
  starting transfers between devices: 32 us -> 0 us
  matrix products: 23.8 us -> 0 us
  waiting for transfers between devices: 16.9 us -> 0 us
  other arithmetic: 7.19 us -> 0 us
  local copies, waits for them, and re-layouts: 11.8 us -> 6.32 us
    psum x6 -> x0, blocking collectives: 199 us -> none  [the longest x3 118 us: norm_of(): return jnp.sqrt(lax.psum(inner(vectors, vectors), 'dom') + epsilon)]
    pallas_call x0 -> x1, Pallas kernels: none -> 36.1 us  [per_device(): pl.pallas_call(functools.partial(kernel, n, radices), out_shape=(jax.Shap...]
    ppermute x14 -> x0, starting transfers between devices: 32 us -> none  [the longest x7 22.8 us: padded(): before = lax.ppermute(last, axis, up)]
    dot_general x9 -> x0, matrix products: 23.8 us -> none  [the longest x3 11.9 us: products(): jnp.einsum('ekij,eri->ekrj', blocks, scaled, preferred_element_type=jnp.f...]
    ppermute x14 -> x0, waiting for transfers between devices: 16.9 us -> none  [the longest x7 15.1 us: padded(): after = lax.ppermute(first, axis, down)]
    unnamed x9 -> x13, local copies, waits for them, and re-layouts: 0.79 us -> 6.32 us
    gather x9 -> x0, local copies, waits for them, and re-layouts: 5.03 us -> none  [the longest x3 1.74 us: products(): beside_all = jnp.take(table, faces, axis=0)]
    scatter x6 -> x0, local copies, waits for them, and re-layouts: 3.61 us -> none  [the longest x3 1.81 us: operate(): prev_part = blank.at[prev_upper].set(lower_terms)]
  transfers between devices with their start and end apart: 14 -> 0, of which waited for: 8 -> 0; matrix products, arithmetic and copies ran while one was open for 2% -> 0% of each run, Pallas kernels for 0% -> 0%
where the time goes in v1:
time: 43.3 us; the launch traced here: 43.1 us
  Pallas kernels  36.1 us (83%)
  local copies, waits for them, and re-layouts  6.32 us (15%)
  between operations  0.71 us (2%)
    pallas_call x1, Pallas kernels, per_device(): pl.pallas_call(functools.partial(kernel, n, radices), out_shape=(jax.Shap...  36.1 us
    unnamed x13, local copies, waits for them, and re-layouts  6.32 us

profile of v1, /device:TPU:0, one launch (start us, length us, event | category | flops | bytes accessed | tf_op | source)
XLA Modules:
  0.0 43.1 jit_solution(127783383658010623)
XLA Ops:
  0.6 1.2 %copy.10.wgt_hbm = bf16[8,162,162]{2,1,0:T(8,128)(2,1)S(1)} copy(bf16[8,162,162]{2,0,1:T(8,128)(2,1)} %param.7) | data formatting | bytes 839808 | tf_op args[1]
  1.9 0.0 copy-start
  1.9 0.0 copy-start.1
  1.9 0.0 copy-start.2
  1.9 0.0 copy-start.3
  1.9 3.3 %copy.9.jac_hbm = bf16[8,7,162,162]{3,2,1,0:T(8,128)(2,1)S(1)} copy(bf16[8,7,162,162]{3,0,2,1:T(8,128)(2,1)} %param.6) | data formatting | bytes 5878656 | tf_op args[0]
  5.2 0.0 copy-done
  5.2 0.0 copy-done.1
  5.2 0.0 copy-done.2
  5.2 0.0 copy-done.3
  5.2 36.1 %shard_map.85 = (f32[8,8,162]{2,1,0:T(8,128)S(1)}, f32[8,8,162]{2,1,0:T(8,128)S(1)}, f32[1,8]{1,0:T(1,128)S(1)}) custom-call(bf16[8,7,162,162]{3,2,1,0:T(8,128)(2,1)S(1)} %copy.9.jac_hbm, bf16[8,162,162]{2,1,0:T(8,128)(2,1)S(1)} %copy.10.wgt_hbm, f32[8,8,162]{2,1,0:T(8,128)S(1)} %copy-done, f32[8,162]{1,0:T(8,128)S(1)} %copy-done.1, s32[8,6]{1,0:T(8,128)S(1)} %copy-done.2, ...), custom_call_target="tpu_custom_call" | custom-call | tf_op jit(solution)/shard_map/pallas_call | solution.py:360
  41.4 0.6 %copy.14 = f32[8,8,162]{2,1,0:T(8,128)} copy(f32[8,8,162]{2,1,0:T(8,128)S(1)} %get-tuple-element.12) | data formatting | bytes 82944
  42.0 0.6 %copy.15 = f32[8,8,162]{2,1,0:T(8,128)} copy(f32[8,8,162]{2,1,0:T(8,128)S(1)} %get-tuple-element.13) | data formatting | bytes 82944
  42.6 0.5 %copy.16 = f32[8]{0:T(128)} copy(f32[8]{0:T(128)S(1)} %bitcast.1) | data formatting | bytes 64
Async XLA Ops:
  1.9 3.4 %copy-start = (f32[8,8,162]{2,1,0:T(8,128)S(1)}, f32[8,8,162]{2,1,0:T(8,128)}, u32[]{:S(2)}) copy-start(f32[8,8,162]{2,1,0:T(8,128)} %rhs_ref.1) | copy-start | bytes 124420
  1.9 3.4 %copy-start.1 = (f32[8,162]{1,0:T(8,128)S(1)}, f32[8,162]{1,0:T(8,128)}, u32[]{:S(2)}) copy-start(f32[8,162]{1,0:T(8,128)} %flow_ref.1) | copy-start | bytes 15556
  1.9 3.3 %copy-start.2 = (s32[8,6]{1,0:T(8,128)S(1)}, s32[8,6]{1,0:T(8,128)}, u32[]{:S(2)}) copy-start(s32[8,6]{1,0:T(8,128)} %nbr_ref.1) | copy-start | bytes 580
  1.9 3.3 %copy-start.3 = (s32[1,2,2]{2,1,0:T(2,128)S(1)}, s32[1,2,2]{2,1,0:T(2,128)}, u32[]{:S(2)}) copy-start(s32[1,2,2]{2,1,0:T(2,128)} %list_ref.1) | copy-start | bytes 52

commit v2 on v1

--- a/solution.py
+++ b/solution.py
@@ -29,10 +29,6 @@
 
 def dot_rows(rows, block):
     return lax.dot_general(rows, block, (((1,), (0,)), ((), ())), preferred_element_type=F32)
-
-
-def dot_rows_t(rows, block):
-    return lax.dot_general(rows, block, (((1,), (1,)), ((), ())), preferred_element_type=F32)
 
 
 def coefficients(beta, b, c, d, e, f, g):
@@ -71,20 +67,21 @@
     n, radices,
     jac_hbm, wgt_hbm, rhs_ref, flow_ref, nbr_ref, list_ref,
     adj_ref, res_ref, ind_ref,
-    jac, wgt, xs, up, hsend, hrecv, asend, arecv, isend, irecv,
+    jraw, wraw, jac, jac_t, wgt_t, left, right, xs, up, hsend, hrecv, asend, arecv, isend, irecv,
     jsem, wsem, hs_sem, hr_sem, as_sem, ar_sem, is_sem, ir_sem,
 ):
-    elements, faces1 = jac.shape[0], jac.shape[1]
+    faces1, elements = jac.shape[0], jac.shape[1]
+    width = jac.shape[2]
+    half = left.shape[1]
     cap = list_ref.shape[2]
     slots = elements + 2 * cap
     me = lax.axis_index("dom")
     core = lax.axis_index("rhs")
     cores = lax.axis_size("rhs")
 
-    jcopies = [pltpu.make_async_copy(jac_hbm.at[e], jac.at[e], jsem.at[e]) for e in range(elements)]
-    wcopy = pltpu.make_async_copy(wgt_hbm, wgt, wsem)
-    for copy in jcopies:
-        copy.start()
+    for k in range(faces1):
+        pltpu.make_async_copy(jac_hbm.at[k], jraw.at[k], jsem.at[k]).start()
+    wcopy = pltpu.make_async_copy(wgt_hbm, wraw, wsem)
     wcopy.start()
 
     strides = []
@@ -98,14 +95,24 @@
         digit = lax.rem(lax.div(me, step), radix)
         return me + (lax.rem(digit + offset, radix) - digit) * step
 
+    stages = len(radices)
+
+    def peers(stage):
+        spread = cores if stage == stages - 1 else 1
+        out = []
+        for offset in range(radices[stage]):
+            for other in range(spread):
+                if offset or other:
+                    target = partner(stage, offset) if offset else me
+                    out.append((offset, other, (target, lax.rem(core + other, cores))))
+        return out
+
     barrier = pltpu.get_barrier_semaphore()
-    total = cores - 1
-    for stage, radix in enumerate(radices):
-        for offset in range(1, radix):
-            pl.semaphore_signal(barrier, inc=1, device_id=(partner(stage, offset), core), device_id_type=MESH)
+    total = 0
+    for stage in range(stages):
+        for _, _, target in peers(stage):
+            pl.semaphore_signal(barrier, inc=1, device_id=target, device_id_type=MESH)
             total += 1
-    for o in range(1, cores):
-        pl.semaphore_signal(barrier, inc=1, device_id=(me, lax.rem(core + o, cores)), device_id_type=MESH)
 
     @pl.when(me > 0)
     def _():
@@ -173,13 +180,13 @@
         return [
             pltpu.make_async_remote_copy(
                 src_ref=asend.at[q, stage],
-                dst_ref=arecv.at[q, stage, o - 1],
-                send_sem=as_sem.at[q, stage, o - 1],
-                recv_sem=ar_sem.at[q, stage, o - 1],
-                device_id=(partner(stage, o), core),
+                dst_ref=arecv.at[q, stage, other, offset],
+                send_sem=as_sem.at[q, stage, other, offset],
+                recv_sem=ar_sem.at[q, stage, other, offset],
+                device_id=target,
                 device_id_type=MESH,
             )
-            for o in range(1, radices[stage])
+            for offset, other, target in peers(stage)
         ]
 
     def reduce_start(q, stage, value):
@@ -190,12 +197,14 @@
     def reduce_end(q, stage):
         for copy in reduce_copies(q, stage):
             copy.wait()
-        value = asend[q, stage]
-        for o in range(1, radices[stage]):
-            value = value + arecv[q, stage, o - 1]
-        return value
-
-    stages = len(radices)
+        sums = []
+        for other in range(cores if stage == stages - 1 else 1):
+            value = arecv[q, stage, other, 0] if other else asend[q, stage]
+            for offset in range(1, radices[stage]):
+                value = value + arecv[q, stage, other, offset]
+            sums.append(value)
+        return sums
+
     lane = lax.broadcasted_iota(jnp.int32, asend.shape[2:], 1)
 
     def packed(columns):
@@ -222,25 +231,46 @@
     halo_start(0)
     reduce_start(0, 0, b_part)
 
-    def forward(t, wait_blocks=False):
+    def spread_rows(raw):
+        left[...] = raw[:, :, 0:half].astype(F32).reshape(left.shape)
+        right[:, 0 : width - half] = (
+            raw[:, :, half:width].astype(F32).reshape(width * elements, width - half)
+        )
+
+    def block_of(e):
+        rows = pl.ds(e, width, stride=elements)
+        return jnp.concatenate([left[rows, :], right[rows, :]], axis=1)
+
+    def take_apart(k, carry):
+        pltpu.make_async_copy(jac_hbm.at[k], jraw.at[k], jsem.at[k]).wait()
+        spread_rows(jraw[k])
+        for e in range(elements):
+            block = block_of(e)[:, 0:width].astype(BF16)
+            jac[k, e] = block
+            jac_t[k, e] = block.T
+        return carry
+
+    lax.fori_loop(0, faces1, take_apart, 0)
+    wcopy.wait()
+    spread_rows(wraw[...])
+    for e in range(elements):
+        wgt_t[e] = block_of(e)[:, 0:width].astype(BF16).T
+
+    def forward(t):
         y = []
         for e in range(elements):
-            if wait_blocks:
-                jcopies[e].wait()
-            acc = dot_rows_t(xs[t, e].astype(BF16), jac[e, 0])
+            acc = dot_rows(xs[t, e].astype(BF16), jac_t[0, e])
             for k in range(1, faces1):
-                acc = acc + dot_rows_t(xs[t, nbr[e][k - 1]].astype(BF16), jac[e, k])
+                acc = acc + dot_rows(xs[t, nbr[e][k - 1]].astype(BF16), jac_t[k, e])
             y.append(acc.astype(BF16))
-        if wait_blocks:
-            wcopy.wait()
-        return [dot_rows_t(y[e], wgt[e]).astype(BF16) for e in range(elements)]
+        return [dot_rows(y[e], wgt_t[e]).astype(BF16) for e in range(elements)]
 
     def backward(z):
         acc = [jnp.zeros(rows_shape, F32) for _ in range(slots)]
         for e in range(elements):
-            acc[e] = acc[e] + dot_rows(z[e], jac[e, 0])
+            acc[e] = acc[e] + dot_rows(z[e], jac[0, e])
             for k in range(1, faces1):
-                term = dot_rows(z[e], jac[e, k])
+                term = dot_rows(z[e], jac[k, e])
                 for m in range(slots):
                     acc[m] = acc[m] + jnp.where(nbr[e][k - 1] == m, term, 0.0)
         return acc
@@ -262,35 +292,55 @@
                 value = value + jnp.where(lists[side][s] == m, hrecv[t, side, cap + s], 0.0)
         return value
 
-    def receive_partials(t):
+    def receive_partials(t, factor=1.0):
         for m in range(elements):
-            xs[t, m] = merged(t, m)
+            xs[t, m] = merged(t, m) * factor
         for side in range(2):
             for s in range(cap):
                 m = elements + side * cap + s
-                xs[t, m] = up[t, m] + hrecv[t, side, s]
+                xs[t, m] = (up[t, m] + hrecv[t, side, s]) * factor
 
     halo_wait(0)
     for side in range(2):
         for s in range(cap):
             xs[0, elements + side * cap + s] = hrecv[0, side, s]
-    z = forward(0, True)
+    send_partials(1, backward(forward(0)))
     for stage in range(stages - 1):
-        reduce_start(0, stage + 1, reduce_end(0, stage))
-    acc = backward(z)
-    b_sum = reduce_end(0, stages - 1)[:, 0:1]
-    beta = jnp.sqrt(b_sum + EPSILON)
-    scale = 1.0 / beta
-    send_partials(1, [a * scale for a in acc])
+        reduce_start(0, stage + 1, reduce_end(0, stage)[0])
     halo_wait(1)
     receive_partials(1)
-    acc = backward(forward(1))
-    send_partials(2, acc)
+    span = range(elements)
+    flow = jnp.zeros(isend.shape, F32)
+    ilane = lax.broadcasted_iota(jnp.int32, isend.shape, 1)
+    for e in span:
+        row = flow_ref[pl.ds(e, 1), :]
+        flow = jnp.where(ilane == e, jnp.sum(rhs_ref[e] * row, axis=1, keepdims=True), flow)
+        flow = jnp.where(
+            ilane == elements + e, jnp.sum(xs[1, e] * row, axis=1, keepdims=True), flow
+        )
+    isend[...] = flow
+    icopies = [
+        pltpu.make_async_remote_copy(
+            src_ref=isend,
+            dst_ref=irecv.at[o - 1],
+            send_sem=is_sem.at[o - 1],
+            recv_sem=ir_sem.at[o - 1],
+            device_id=(me, lax.rem(core + o, cores)),
+            device_id_type=MESH,
+        )
+        for o in range(1, cores)
+    ]
+    for copy in icopies:
+        copy.start()
+    send_partials(2, backward(forward(1)))
+    b_sums = [v[:, 0:1] for v in reduce_end(0, stages - 1)]
+    betas = [jnp.sqrt(v + EPSILON) for v in b_sums]
+    scales = [1.0 / v for v in betas]
+    scale = scales[0]
+    v1 = [rhs_ref[e] * scale for e in span]
+    raw = [xs[1, e] * scale for e in span]
     halo_wait(2)
-    receive_partials(2)
-    span = range(elements)
-    v1 = [rhs_ref[e] * scale for e in span]
-    raw = [xs[1, e] for e in span]
+    receive_partials(2, scale)
     u2 = [xs[2, e] for e in span]
     grams = packed(
         [
@@ -302,52 +352,38 @@
         ]
     )
     reduce_start(1, 0, grams)
-    z = forward(2)
+    send_partials(3, backward(forward(2)))
     for stage in range(stages - 1):
-        reduce_start(1, stage + 1, reduce_end(1, stage))
-    acc = backward(z)
-    send_partials(3, acc)
-    sums = reduce_end(1, stages - 1)
-    c, d, e_, f, g = [sums[:, i : i + 1] for i in range(5)]
-    a0, a1 = coefficients(beta, b_sum * scale * scale, c, d, e_, f, g)
-    a0s = a0 * scale
-    ind = jnp.zeros(isend.shape[1:], F32)
-    ilane = lax.broadcasted_iota(jnp.int32, isend.shape[1:], 1)
+        reduce_start(1, stage + 1, reduce_end(1, stage)[0])
+    all_sums = reduce_end(1, stages - 1)
+    for copy in icopies:
+        copy.wait()
+    ind = None
+    for o in range(cores):
+        sums = [all_sums[o][:, i : i + 1] for i in range(5)]
+        a0, a1 = coefficients(betas[o], b_sums[o] * scales[o] * scales[o], *sums)
+        flow = isend[...] if o == 0 else irecv[o - 1]
+        dots = a0 * scales[o] * flow[:, 0:elements] + a1 * scales[o] * flow[:, elements : 2 * elements]
+        term = jnp.sum(jnp.abs(dots), axis=0, keepdims=True)
+        ind = term if ind is None else ind + term
+        if o == 0:
+            own0, own1 = a0, a1
+    ind_ref[...] = ind
+    k0 = own0 * scale
+    k1 = own1 * scale
     for e in span:
-        adjoint = a0s * rhs_ref[e] + a1 * xs[1, e]
-        adj_ref[e] = adjoint
-        term = jnp.abs(jnp.sum(adjoint * flow_ref[pl.ds(e, 1), :], axis=1, keepdims=True))
-        ind = jnp.where(ilane == e, jnp.sum(term, axis=0, keepdims=True), ind)
-    isend[0] = ind
-    icopies = [
-        pltpu.make_async_remote_copy(
-            src_ref=isend.at[0],
-            dst_ref=irecv.at[o - 1],
-            send_sem=is_sem.at[o - 1],
-            recv_sem=ir_sem.at[o - 1],
-            device_id=(me, lax.rem(core + o, cores)),
-            device_id_type=MESH,
-        )
-        for o in range(1, cores)
-    ]
-    for copy in icopies:
-        copy.start()
-    k1 = beta + a0
-    k2 = a1 - a0
+        adj_ref[e] = k0 * rhs_ref[e] + k1 * xs[1, e]
+    k1 = 1.0 + k0
+    k2 = own1 - own0
     halo_wait(3)
     for e in span:
-        res_ref[e] = rhs_ref[e] - (k1 * xs[1, e] + k2 * xs[2, e] - a1 * merged(3, e))
-    for copy in icopies:
-        copy.wait()
-    for o in range(1, cores):
-        ind = ind + irecv[o - 1]
-    ind_ref[...] = ind[0:1, 0:elements]
+        res_ref[e] = rhs_ref[e] - (k1 * xs[1, e] + k2 * xs[2, e] - own1 * merged(3, e))
     for t in range(4):
         halo_finish(t)
 
 
 def per_device(n, jacobian, block_weight, rhs_grad, flow_residual, face_nbr, send_list):
-    elements = jacobian.shape[0]
+    elements, faces1, width = jacobian.shape[:3]
     rows = rhs_grad.shape[1:]
     cap = send_list.shape[2]
     slots = elements + 2 * cap
@@ -367,29 +403,35 @@
         in_specs=[anywhere, anywhere, vmem, vmem, smem, smem],
         out_specs=(vmem, vmem, vmem),
         scratch_shapes=[
-            pltpu.VMEM(jacobian.shape, BF16),
-            pltpu.VMEM(block_weight.shape, BF16),
+            pltpu.VMEM((faces1, width, elements, width), BF16),
+            pltpu.VMEM((width, elements, width), BF16),
+            pltpu.VMEM((faces1, elements, width, width), BF16),
+            pltpu.VMEM((faces1, elements, width, width), BF16),
+            pltpu.VMEM((elements, width, width), BF16),
+            pltpu.VMEM((width * elements, 128), F32),
+            pltpu.VMEM((width * elements, 128), F32),
             pltpu.VMEM((3, slots) + rows, F32),
             pltpu.VMEM((4, slots) + rows, F32),
             pltpu.VMEM((4, 2, 2 * cap) + rows, F32),
             pltpu.VMEM((4, 2, 2 * cap) + rows, F32),
             pltpu.VMEM((2, stages, rows[0], 128), F32),
-            pltpu.VMEM((2, stages, widest - 1, rows[0], 128), F32),
-            pltpu.VMEM((1, 8, 128), F32),
-            pltpu.VMEM((max(cores - 1, 1), 8, 128), F32),
-            pltpu.SemaphoreType.DMA((elements,)),
+            pltpu.VMEM((2, stages, cores, widest, rows[0], 128), F32),
+            pltpu.VMEM((rows[0], 128), F32),
+            pltpu.VMEM((max(cores - 1, 1), rows[0], 128), F32),
+            pltpu.SemaphoreType.DMA((faces1,)),
             pltpu.SemaphoreType.DMA,
             pltpu.SemaphoreType.DMA((4, 2)),
             pltpu.SemaphoreType.DMA((4, 2)),
-            pltpu.SemaphoreType.DMA((2, stages, widest - 1)),
-            pltpu.SemaphoreType.DMA((2, stages, widest - 1)),
+            pltpu.SemaphoreType.DMA((2, stages, cores, widest)),
+            pltpu.SemaphoreType.DMA((2, stages, cores, widest)),
             pltpu.SemaphoreType.DMA((max(cores - 1, 1),)),
             pltpu.SemaphoreType.DMA((max(cores - 1, 1),)),
         ],
         compiler_params=pltpu.CompilerParams(
-            collective_id=0, has_side_effects=True, vmem_limit_bytes=40 * 2**20
+            collective_id=0, has_side_effects=True, vmem_limit_bytes=56 * 2**20
         ),
-    )(jacobian, block_weight, rhs_grad, flow_residual, face_nbr, send_list)
+    )(
+        jnp.transpose(jacobian, (1, 2, 0, 3)), jnp.transpose(block_weight, (1, 0, 2)), rhs_grad, flow_residual, face_nbr, send_list)
     return adjoint, residual, indicator.reshape(elements)
 
 

time: 43.3 us -> 34.5 us (0.80)
  Pallas kernels: 36.1 us -> 29.5 us
  local copies, waits for them, and re-layouts: 6.32 us -> 4.12 us
    pallas_call x1, Pallas kernels: 36.1 us -> 29.5 us  [per_device(): pl.pallas_call(functools.partial(kernel, n, radices), out_shape=(jax.Shap...]
    unnamed x13 -> x3, local copies, waits for them, and re-layouts: 6.32 us -> 4.12 us
where the time goes in v2:
time: 34.5 us; the launch traced here: 34.2 us
  Pallas kernels  29.5 us (86%)
  local copies, waits for them, and re-layouts  4.12 us (12%)
  between operations  0.64 us (2%)
    pallas_call x1, Pallas kernels, per_device(): pl.pallas_call(functools.partial(kernel, n, radices), out_shape=(jax.Shap...  29.5 us
    unnamed x3, local copies, waits for them, and re-layouts  4.12 us

profile of v2, /device:TPU:0, one launch (start us, length us, event | category | flops | bytes accessed | tf_op | source)
XLA Modules:
  0.0 34.2 jit_solution(7524906797351407575)
XLA Ops:
  0.6 29.5 %shard_map.85 = (f32[8,8,162]{2,1,0:T(8,128)}, f32[8,8,162]{2,1,0:T(8,128)}, f32[1,8]{1,0:T(1,128)}) custom-call(bf16[7,162,8,162]{3,2,1,0:T(8,128)(2,1)} %bitcast.3, bf16[162,8,162]{2,1,0:T(8,128)(2,1)} %bitcast.4, f32[8,8,162]{2,1,0:T(8,128)} %rhs_ref.1, f32[8,162]{1,0:T(8,128)} %flow_ref.1, s32[8,6]{1,0:T(8,128)} %nbr_ref.1, s32[1,2,2]{2,1,0:T(2,128)} %list_ref.1), custom_call_target="tpu_custom_call" | custom-call | tf_op jit(solution)/shard_map/pallas_call | solution.py:396
  30.1 1.5 %copy.12 = f32[8,8,162]{2,1,0:T(8,128)} copy(f32[8,8,162]{2,1,0:T(8,128)} %get-tuple-element.12) | data formatting | bytes 82944
  31.6 1.5 %copy.13 = f32[8,8,162]{2,1,0:T(8,128)} copy(f32[8,8,162]{2,1,0:T(8,128)} %get-tuple-element.13) | data formatting | bytes 82944
  33.0 1.2 %copy.14 = f32[8]{0:T(128)} copy(f32[8]{0:T(128)} %bitcast.5) | data formatting | bytes 64

commit v3 on v2

--- a/solution.py
+++ b/solution.py
@@ -8,6 +8,7 @@
 from jax.sharding import PartitionSpec as P
 
 EPSILON = 1e-06
+EARLY = 2
 MESH = pl.DeviceIdType.MESH
 F32 = jnp.float32
 BF16 = jnp.bfloat16
@@ -124,18 +125,22 @@
 
     rows_shape = rhs_ref.shape[1:]
 
+    height = rows_shape[0]
+    blank = jnp.zeros((hrecv.shape[0],) + hrecv.shape[2:], BF16)
+
     @pl.when(me == 0)
     def _():
-        hrecv[:, 0] = jnp.zeros((4, 2 * cap) + rows_shape, F32)
+        hrecv[:, 0] = blank
 
     @pl.when(me == n - 1)
     def _():
-        hrecv[:, 1] = jnp.zeros((4, 2 * cap) + rows_shape, F32)
+        hrecv[:, 1] = blank
 
     lists = [[list_ref[0, side, s] for s in range(cap)] for side in range(2)]
     nbr = [[nbr_ref[e, k] for k in range(faces1 - 1)] for e in range(elements)]
 
-    ranges = ((0, cap), (0, 2 * cap), (0, 2 * cap), (cap, cap))
+    part = cap * height
+    ranges = ((0, part), (0, 2 * part), (0, 2 * part), (part, part))
 
     def halo(t, side):
         first, count = ranges[t]
@@ -222,14 +227,10 @@
     r = [rhs_ref[e] for e in range(elements)]
     b_part = packed([inner([(v, v) for v in r])])
     for side in range(2):
-        for s in range(cap):
-            hsend[0, side, s] = rhs_ref[lists[side][s]]
+        chosen = [rhs_ref[lists[side][s]] for s in range(cap)]
+        hsend[0, side, 0:part] = jnp.concatenate(chosen, axis=0).astype(BF16)
     for e in range(elements):
         xs[0, e] = r[e]
-
-    pl.semaphore_wait(barrier, total + jnp.where(me > 0, 1, 0) + jnp.where(me < n - 1, 1, 0))
-    halo_start(0)
-    reduce_start(0, 0, b_part)
 
     def spread_rows(raw):
         left[...] = raw[:, :, 0:half].astype(F32).reshape(left.shape)
@@ -250,7 +251,12 @@
             jac_t[k, e] = block.T
         return carry
 
-    lax.fori_loop(0, faces1, take_apart, 0)
+    lax.fori_loop(0, EARLY, take_apart, 0)
+    pl.semaphore_wait(barrier, total + jnp.where(me > 0, 1, 0) + jnp.where(me < n - 1, 1, 0))
+    halo_start(0)
+    reduce_start(0, 0, b_part)
+
+    lax.fori_loop(EARLY, faces1, take_apart, 0)
     wcopy.wait()
     spread_rows(wraw[...])
     for e in range(elements):
@@ -279,31 +285,38 @@
         for m in range(slots):
             up[t, m] = acc[m]
         for side in range(2):
-            for s in range(cap):
-                if t < 3:
-                    hsend[t, side, s] = up[t, lists[side][s]]
-                hsend[t, side, cap + s] = acc[elements + side * cap + s]
+            first = elements + side * cap
+            terms = jnp.concatenate(acc[first : first + cap], axis=0)
+            hsend[t, side, part : 2 * part] = terms.astype(BF16)
+            if t < 3:
+                owned = jnp.concatenate([up[t, lists[side][s]] for s in range(cap)], axis=0)
+                hsend[t, side, 0:part] = owned.astype(BF16)
         halo_start(t)
 
-    def merged(t, m):
-        value = up[t, m]
+    def arrived(t, side, first):
+        rows = hrecv[t, side, first : first + part].astype(F32)
+        return [rows[s * height : (s + 1) * height] for s in range(cap)]
+
+    def merged(t):
+        values = [up[t, m] for m in range(elements)]
         for side in range(2):
-            for s in range(cap):
-                value = value + jnp.where(lists[side][s] == m, hrecv[t, side, cap + s], 0.0)
-        return value
+            for s, term in enumerate(arrived(t, side, part)):
+                for m in range(elements):
+                    values[m] = values[m] + jnp.where(lists[side][s] == m, term, 0.0)
+        return values
 
     def receive_partials(t, factor=1.0):
-        for m in range(elements):
-            xs[t, m] = merged(t, m) * factor
+        for m, value in enumerate(merged(t)):
+            xs[t, m] = value * factor
         for side in range(2):
-            for s in range(cap):
+            for s, term in enumerate(arrived(t, side, 0)):
                 m = elements + side * cap + s
-                xs[t, m] = (up[t, m] + hrecv[t, side, s]) * factor
+                xs[t, m] = (up[t, m] + term) * factor
 
     halo_wait(0)
     for side in range(2):
-        for s in range(cap):
-            xs[0, elements + side * cap + s] = hrecv[0, side, s]
+        for s, term in enumerate(arrived(0, side, 0)):
+            xs[0, elements + side * cap + s] = term
     send_partials(1, backward(forward(0)))
     for stage in range(stages - 1):
         reduce_start(0, stage + 1, reduce_end(0, stage)[0])
@@ -376,10 +389,19 @@
     k1 = 1.0 + k0
     k2 = own1 - own0
     halo_wait(3)
-    for e in span:
-        res_ref[e] = rhs_ref[e] - (k1 * xs[1, e] + k2 * xs[2, e] - own1 * merged(3, e))
+    for e, value in enumerate(merged(3)):
+        res_ref[e] = rhs_ref[e] - (k1 * xs[1, e] + k2 * xs[2, e] - own1 * value)
     for t in range(4):
         halo_finish(t)
+
+
+def write_out(a_in, b_in, c_in, a_out, b_out, c_out, sems):
+    pairs = ((a_in, a_out), (b_in, b_out), (c_in, c_out))
+    copies = [pltpu.make_async_copy(src, dst, sems.at[i]) for i, (src, dst) in enumerate(pairs)]
+    for copy in copies:
+        copy.start()
+    for copy in copies:
+        copy.wait()
 
 
 def per_device(n, jacobian, block_weight, rhs_grad, flow_residual, face_nbr, send_list):
@@ -392,7 +414,7 @@
     cores = lax.axis_size("rhs")
     vmem = pl.BlockSpec(memory_space=pltpu.VMEM)
     smem = pl.BlockSpec(memory_space=pltpu.SMEM)
-    anywhere = pl.BlockSpec(memory_space=pl.ANY)
+    anywhere = pl.BlockSpec(memory_space=pltpu.HBM)
     adjoint, residual, indicator = pl.pallas_call(
         functools.partial(kernel, n, radices),
         out_shape=(
@@ -412,8 +434,8 @@
             pltpu.VMEM((width * elements, 128), F32),
             pltpu.VMEM((3, slots) + rows, F32),
             pltpu.VMEM((4, slots) + rows, F32),
-            pltpu.VMEM((4, 2, 2 * cap) + rows, F32),
-            pltpu.VMEM((4, 2, 2 * cap) + rows, F32),
+            pltpu.VMEM((4, 2, 2 * cap * rows[0], width), BF16),
+            pltpu.VMEM((4, 2, 2 * cap * rows[0], width), BF16),
             pltpu.VMEM((2, stages, rows[0], 128), F32),
             pltpu.VMEM((2, stages, cores, widest, rows[0], 128), F32),
             pltpu.VMEM((rows[0], 128), F32),
@@ -428,10 +450,19 @@
             pltpu.SemaphoreType.DMA((max(cores - 1, 1),)),
         ],
         compiler_params=pltpu.CompilerParams(
-            collective_id=0, has_side_effects=True, vmem_limit_bytes=56 * 2**20
+            collective_id=0, has_side_effects=True, vmem_limit_bytes=50 * 2**20
         ),
     )(
         jnp.transpose(jacobian, (1, 2, 0, 3)), jnp.transpose(block_weight, (1, 0, 2)), rhs_grad, flow_residual, face_nbr, send_list)
+    results = (adjoint, residual, indicator)
+    adjoint, residual, indicator = pl.pallas_call(
+        write_out,
+        out_shape=tuple(jax.ShapeDtypeStruct(v.shape, F32) for v in results),
+        in_specs=[pl.BlockSpec(memory_space=pl.ANY)] * 3,
+        out_specs=(anywhere,) * 3,
+        scratch_shapes=[pltpu.SemaphoreType.DMA((3,))],
+        compiler_params=pltpu.CompilerParams(vmem_limit_bytes=2 * 2**20),
+    )(*results)
     return adjoint, residual, indicator.reshape(elements)
 
 

time: 34.5 us -> 33.9 us (0.983)
  Pallas kernels: 29.5 us -> 28.9 us
    pallas_call x1, Pallas kernels: 29.5 us -> 28.2 us  [per_device(): pl.pallas_call(functools.partial(kernel, n, radices), out_shape=(jax.Shap...]
    pallas_call x0 -> x1, Pallas kernels: none -> 0.68 us  [per_device(): pl.pallas_call(write_out, out_shape=tuple((jax.ShapeDtypeStruct(v.shape,...]
    unnamed x3 -> x10, local copies, waits for them, and re-layouts: 4.12 us -> 3.98 us
where the time goes in v3:
time: 33.9 us; the launch traced here: 33.6 us
  Pallas kernels  28.9 us (85%)
  local copies, waits for them, and re-layouts  3.98 us (12%)
  between operations  0.65 us (2%)
    pallas_call x1, Pallas kernels, per_device(): pl.pallas_call(functools.partial(kernel, n, radices), out_shape=(jax.Shap...  28.2 us
    unnamed x10, local copies, waits for them, and re-layouts  3.98 us
    pallas_call x1, Pallas kernels, per_device(): pl.pallas_call(write_out, out_shape=tuple((jax.ShapeDtypeStruct(v.shape,...  0.68 us

profile of v3, /device:TPU:0, one launch (start us, length us, event | category | flops | bytes accessed | tf_op | source)
XLA Modules:
  0.0 33.6 jit_solution(7309388997119164834)
XLA Ops:
  0.6 0.0 copy-start
  0.6 1.1 %copy-done = bf16[8,162,162]{2,0,1:T(8,128)(2,1)S(1)} copy-done((bf16[8,162,162]{2,0,1:T(8,128)(2,1)S(1)}, bf16[8,162,162]{2,0,1:T(8,128)(2,1)}, u32[]{:S(2)}) %copy-start) | copy-done | bytes 419928
  1.7 0.0 copy-start.1
  1.7 0.8 %copy-done.1 = f32[8,8,162]{2,1,0:T(8,128)S(1)} copy-done((f32[8,8,162]{2,1,0:T(8,128)S(1)}, f32[8,8,162]{2,1,0:T(8,128)}, u32[]{:S(2)}) %copy-start.1) | copy-done | bytes 41496
  2.6 0.0 copy-start.2
  2.6 0.7 %copy-done.2 = f32[8,162]{1,0:T(8,128)S(1)} copy-done((f32[8,162]{1,0:T(8,128)S(1)}, f32[8,162]{1,0:T(8,128)}, u32[]{:S(2)}) %copy-start.2) | copy-done | bytes 5208
  3.3 0.0 copy-start.3
  3.3 0.7 %copy-done.3 = s32[8,6]{1,0:T(8,128)S(1)} copy-done((s32[8,6]{1,0:T(8,128)S(1)}, s32[8,6]{1,0:T(8,128)}, u32[]{:S(2)}) %copy-start.3) | copy-done | bytes 216
  3.9 0.0 copy-start.4
  4.0 0.7 %copy-done.4 = s32[1,2,2]{2,1,0:T(2,128)S(1)} copy-done((s32[1,2,2]{2,1,0:T(2,128)S(1)}, s32[1,2,2]{2,1,0:T(2,128)}, u32[]{:S(2)}) %copy-start.4) | copy-done | bytes 40
  4.6 28.2 %shard_map.85 = (f32[8,8,162]{2,1,0:T(8,128)S(1)}, f32[8,8,162]{2,1,0:T(8,128)S(1)}, f32[1,8]{1,0:T(1,128)S(1)}) custom-call(bf16[7,162,8,162]{3,2,1,0:T(8,128)(2,1)} %bitcast.4, bf16[162,8,162]{2,1,0:T(8,128)(2,1)S(1)} %bitcast.3, f32[8,8,162]{2,1,0:T(8,128)S(1)} %copy-done.1, f32[8,162]{1,0:T(8,128)S(1)} %copy-done.2, s32[8,6]{1,0:T(8,128)S(1)} %copy-done.3, ...), custom_call_target="tpu_custom_call" | custom-call | tf_op jit(solution)/shard_map/pallas_call | solution.py:418
  32.9 0.7 %shard_map.86 = (f32[8,8,162]{2,1,0:T(8,128)}, f32[8,8,162]{2,1,0:T(8,128)}, f32[1,8]{1,0:T(1,128)}) custom-call(f32[8,8,162]{2,1,0:T(8,128)S(1)} %get-tuple-element.9.a_in, f32[8,8,162]{2,1,0:T(8,128)S(1)} %get-tuple-element.10.b_in, f32[1,8]{1,0:T(1,128)S(1)} %get-tuple-element.11.c_in), custom_call_target="tpu_custom_call" | custom-call | tf_op jit(solution)/shard_map/pallas_call | solution.py:458
Async XLA Ops:
  0.6 1.1 %copy-start = (bf16[8,162,162]{2,0,1:T(8,128)(2,1)S(1)}, bf16[8,162,162]{2,0,1:T(8,128)(2,1)}, u32[]{:S(2)}) copy-start(bf16[8,162,162]{2,0,1:T(8,128)(2,1)} %param.7) | copy-start | bytes 1259716
  1.7 0.8 %copy-start.1 = (f32[8,8,162]{2,1,0:T(8,128)S(1)}, f32[8,8,162]{2,1,0:T(8,128)}, u32[]{:S(2)}) copy-start(f32[8,8,162]{2,1,0:T(8,128)} %rhs_ref.1) | copy-start | bytes 124420
  2.6 0.7 %copy-start.2 = (f32[8,162]{1,0:T(8,128)S(1)}, f32[8,162]{1,0:T(8,128)}, u32[]{:S(2)}) copy-start(f32[8,162]{1,0:T(8,128)} %flow_ref.1) | copy-start | bytes 15556
  3.3 0.7 %copy-start.3 = (s32[8,6]{1,0:T(8,128)S(1)}, s32[8,6]{1,0:T(8,128)}, u32[]{:S(2)}) copy-start(s32[8,6]{1,0:T(8,128)} %nbr_ref.1) | copy-start | bytes 580
  3.9 0.7 %copy-start.4 = (s32[1,2,2]{2,1,0:T(2,128)S(1)}, s32[1,2,2]{2,1,0:T(2,128)}, u32[]{:S(2)}) copy-start(s32[1,2,2]{2,1,0:T(2,128)} %list_ref.1) | copy-start | bytes 52
